TPU v7x, 256 devices: a whole 4x4x8 slice. The times are simulated.
256 devices in a mesh: tm: 16 (over z, core), rows: 16 (over y, x).
Axes of the slice: x: 4, y: 4, z: 8, core: 2. Of those that a mesh axis runs over, the one named last changes fastest.
Arguments:
- feats: bfloat16 [32, 32, 96, 640], P('tm', 'rows'), may hold values from -30 to 30, as said below
- norm_gain_vector: float32 [96], replicated, may hold values from 0.25 to 1.75
- conv_weight: bfloat16 [96, 2592], replicated, may hold values from -0.125 to 0.125
- out_gain: float32 [96], replicated, may hold values from 0.25 to 1.75
- rgb_weight: float32 [3, 96], replicated, may hold values from -0.625 to 0.625
- target: float32 [32, 32, 3, 640], P('tm', 'rows'), may hold values from -6 to 6
- pix_weight: float32 [32, 32, 3, 640], P('tm', 'rows'), may hold values from 0.5 to 60, as said below
- frame_seg: int32 [32], replicated, may hold values from 0 to 2, never falling along the last dimension, each value on 1 to 16 neighbouring positions
Outputs:
- grad_feats: bfloat16 [32, 32, 96, 640], P('tm', 'rows')
Inputs may be any that keep to these rules, and one draw needn't show every extreme that they name: `feats`: finite values of order one to a few tens; their spread differs from frame to frame and row to row. `pix_weight`: positive weights. `frame_seg`: segments are runs of consecutive frames numbered from 0 upward.
All inputs are finite; a program needn't handle non-finite values.
Results may differ from a plain program's by a relative error of at most 0.0038.
Values may be sent and summed in bfloat16 or wider, within the bound.
A program may use at most 64 MiB of HBM per device.

v0:
```python
import jax
import jax.numpy as jnp
from jax import lax
from jax.sharding import PartitionSpec as P

EPS = 1e-06
DELTA = 1.0


def from_behind(block, axis, distance):
    devices = range(lax.axis_size(axis))
    route = [(i - distance, i) for i in devices if i - distance in devices]
    return lax.ppermute(block, axis, route)


def extended(cells, sides, width):
    for axis, dim in sides:
        count = lax.axis_size(axis)
        ends = count - 1
        head = lax.slice_in_dim(cells, 0, width, axis=dim)
        tail = lax.slice_in_dim(cells, cells.shape[dim] - width, cells.shape[dim], axis=dim)
        cells = jnp.concatenate(
            [
                lax.ppermute(tail, axis, [(i, (i + 1) % count) for i in range(ends)]),
                cells,
                lax.ppermute(head, axis, [((i + 1) % count, i) for i in range(ends)]),
            ],
            axis=dim,
        )
    return cells


def apply_rms_norm(source, norm_gain_vector):
    pixel_values = source.astype(jnp.float32)
    inverse_std_dev = lax.rsqrt(jnp.mean(pixel_values * pixel_values, axis=2, keepdims=True) + EPS)
    normalized_input = pixel_values * inverse_std_dev
    scaled_normalized = normalized_input * norm_gain_vector[:, None]
    return (
        jax.nn.silu(scaled_normalized).astype(jnp.bfloat16),
        normalized_input,
        scaled_normalized,
        inverse_std_dev,
    )


def local(
    feats, norm_gain_vector, conv_weight, out_gain, rgb_weight, target, pix_weight, frame_seg
):
    frames, rows, chans, width = feats.shape
    entries = lax.axis_size("tm") * frames * lax.axis_size("rows") * rows * 3 * width
    tm_index = lax.axis_index("tm")
    weight_sum = lax.psum(jnp.sum(pix_weight), ("tm", "rows"))
    input_float = feats.astype(jnp.float32)
    activated_input, normalized_input, scaled_normalized, inverse_std_dev = apply_rms_norm(
        feats, norm_gain_vector
    )
    earlier = from_behind(activated_input, "tm", 1)
    act_ext = extended(jnp.concatenate([earlier, activated_input], 0), (("rows", 1),), 1)
    act_pad = jnp.pad(act_ext, ((0, 0), (0, 0), (0, 0), (1, 1)))
    minus = jnp.full((2,), -1, jnp.int32)
    seg_padded = jnp.concatenate([minus, frame_seg, minus])
    seg_ext = lax.dynamic_slice_in_dim(seg_padded, tm_index * frames, frames + 4)
    valid = jnp.stack(
        [seg_ext[i : i + frames + 2] == seg_ext[2 : frames + 4] for i in range(3)], 1
    ).astype(jnp.float32)
    conv_out = jnp.zeros((frames, rows, chans, width), jnp.float32)
    for i in range(3):
        part_sum = jnp.zeros((frames, rows, chans, width), jnp.float32)
        for j in range(3):
            for l in range(3):
                tap_index = (i * 3 + j) * 3 + l
                w_tap = conv_weight[:, tap_index * chans : (tap_index + 1) * chans]
                piece = act_pad[i : i + frames, j : j + rows, :, l : l + width]
                part_sum = part_sum + jnp.einsum(
                    "oc,frcw->frow", w_tap, piece, preferred_element_type=jnp.float32
                )
        conv_out = conv_out + valid[:frames, i][:, None, None, None] * part_sum
    y_full = input_float + conv_out
    out_rstd = lax.rsqrt(jnp.mean(y_full * y_full, axis=2, keepdims=True) + EPS)
    out_hat = y_full * out_rstd
    out_scaled = out_hat * out_gain[:, None]
    out_act = jax.nn.silu(out_scaled)
    rgb = jnp.einsum("ec,frcw->frew", rgb_weight, out_act, precision=lax.Precision.HIGHEST)
    g_rgb = pix_weight * jnp.clip(rgb - target, -DELTA, DELTA) * (entries / weight_sum)
    grad_act_out = jnp.einsum("ec,frew->frcw", rgb_weight, g_rgb, precision=lax.Precision.HIGHEST)
    out_sigma = jax.nn.sigmoid(out_scaled)
    out_term = grad_act_out * out_sigma * (1.0 + out_scaled * (1.0 - out_sigma)) * out_gain[:, None]
    out_proj = jnp.mean(out_term * out_hat, axis=2, keepdims=True)
    output_gradient = out_rstd * (out_term - out_hat * out_proj)
    g_yb = output_gradient.astype(jnp.bfloat16)
    later = from_behind(g_yb, "tm", -1)
    grad_band = extended(jnp.concatenate([g_yb, later], 0), (("rows", 1),), 1)
    grad_pad = jnp.pad(grad_band, ((0, 0), (0, 0), (0, 0), (1, 1)))
    g_act = jnp.zeros((frames, rows, chans, width), jnp.float32)
    for i in range(3):
        part_sum = jnp.zeros((frames, rows, chans, width), jnp.float32)
        for j in range(3):
            for l in range(3):
                tap_index = (i * 3 + j) * 3 + l
                w_tap = conv_weight[:, tap_index * chans : (tap_index + 1) * chans]
                piece = grad_pad[
                    2 - i : 2 - i + frames, 2 - j : 2 - j + rows, :, 2 - l : 2 - l + width
                ]
                part_sum = part_sum + jnp.einsum(
                    "oc,frow->frcw", w_tap, piece, preferred_element_type=jnp.float32
                )
        g_act = g_act + valid[2 - i : 2 - i + frames, i][:, None, None, None] * part_sum
    sigma = jax.nn.sigmoid(scaled_normalized)
    correction_term = (
        g_act * sigma * (1.0 + scaled_normalized * (1.0 - sigma)) * norm_gain_vector[:, None]
    )
    projected_output = jnp.mean(correction_term * normalized_input, axis=2, keepdims=True)
    input_gradient = output_gradient + inverse_std_dev * (
        correction_term - normalized_input * projected_output
    )
    return input_gradient.astype(jnp.bfloat16)


def solution(mesh):
    placed = (
        P("tm", "rows", None, None),
        P(),
        P(),
        P(),
        P(),
        P("tm", "rows", None, None),
        P("tm", "rows", None, None),
        P(),
    )
    return jax.shard_map(
        local, mesh=mesh, in_specs=placed, out_specs=P("tm", "rows", None, None), check_vma=False
    )
```

profile of v0, /device:TPU:57, one launch (start us, length us, event | category | flops | bytes accessed | tf_op | source)
XLA Modules:
  0.0 163.9 jit_solution(6076820253720184006)
XLA Ops:
  0.0 1.2 fusion.79
  1.2 1.5 fusion.72
  2.7 4.1 %collective-permute-start = (bf16[2,2,96,640]{3,2,1,0:T(8,128)(2,1)S(1)}, bf16[2,2,96,640]{3,2,1,0:T(8,128)(2,1)S(1)}, u32[]{:S(2)}, u32[]{:S(2)}) collective-permute-start(bf16[2,2,96,640]{3,2,1,0:T(8,128)(2,1)S(1)} %fusion.72), channel_id=1, source_target_pairs={{0,16},{16,32},{32,48},{48,64},{64,80},{80,96},{96,112},{112,128},... | collective-permute-start | bytes 1474568 | tf_op jit(solution)/shard_map/ppermute | solution.py:13
  6.8 0.7 pad_add_fusion
  7.8 1.4 reduce_sum.47
  9.2 76.5 %psum.7 = f32[]{:T(128)} all-reduce(f32[]{:T(128)} %reduce_sum.47), channel_id=1, replica_groups=mesh['tm'=16,'rows'=16] {'tm','rows'}, use_global_device_ids=true, to_apply=%region_3.4 | all-reduce | flops 1 | bytes 8 | tf_op jit(solution)/shard_map/psum | solution.py:52
  86.5 1.1 fusion.185
  87.8 2.5 %collective-permute-start.2 = (bf16[4,1,96,640]{3,2,1,0:T(8,128)(2,1)S(1)}, bf16[4,1,96,640]{3,2,1,0:T(8,128)(2,1)S(1)}, u32[]{:S(2)}, u32[]{:S(2)}) collective-permute-start(bf16[4,1,96,640]{3,2,1,0:T(8,128)(2,1)S(1)} %get-tuple-element.10), channel_id=1, source_target_pairs={{1,0},{2,1},{3,2},{4,3},{5,4},{6,5},{7,6},{8,7},{9,8},{10,9},{11,1... | collective-permute-start | bytes 1474568 | tf_op jit(solution)/shard_map/ppermute | solution.py:26
  90.3 2.7 %collective-permute-start.1 = (bf16[4,1,96,640]{3,2,1,0:T(8,128)(2,1)S(1)}, bf16[4,1,96,640]{3,2,1,0:T(8,128)(2,1)S(1)}, u32[]{:S(2)}, u32[]{:S(2)}) collective-permute-start(bf16[4,1,96,640]{3,2,1,0:T(8,128)(2,1)S(1)} %get-tuple-element.9), channel_id=1, source_target_pairs={{0,1},{1,2},{2,3},{3,4},{4,5},{5,6},{6,7},{7,8},{8,9},{9,10},{10,1... | collective-permute-start | bytes 1474568 | tf_op jit(solution)/shard_map/ppermute | solution.py:24
  93.7 8.0 %collective-permute-done.2 = bf16[4,1,96,640]{3,2,1,0:T(8,128)(2,1)S(1)} collective-permute-done((bf16[4,1,96,640]{3,2,1,0:T(8,128)(2,1)S(1)}, bf16[4,1,96,640]{3,2,1,0:T(8,128)(2,1)S(1)}, u32[]{:S(2)}, u32[]{:S(2)}) %collective-permute-start.2) | collective-permute-done | bytes 491552 | tf_op jit(solution)/shard_map/ppermute | solution.py:26
  101.8 4.3 %collective-permute-done.1 = bf16[4,1,96,640]{3,2,1,0:T(8,128)(2,1)S(1)} collective-permute-done((bf16[4,1,96,640]{3,2,1,0:T(8,128)(2,1)S(1)}, bf16[4,1,96,640]{3,2,1,0:T(8,128)(2,1)S(1)}, u32[]{:S(2)}, u32[]{:S(2)}) %collective-permute-start.1) | collective-permute-done | bytes 491552 | tf_op jit(solution)/shard_map/ppermute | solution.py:24
  106.1 1.8 %select_maximum_fusion.3 = bf16[4,4,96,642]{3,2,1,0:T(8,128)(2,1)S(1)} fusion(bf16[4,1,96,640]{3,2,1,0:T(8,128)(2,1)S(1)} %collective-permute-done.2, bf16[4,1,96,640]{3,2,1,0:T(8,128)(2,1)S(1)} %collective-permute-done.1, bf16[2,2,96,640]{3,2,1,0:T(8,128)(2,1)S(1)} %fusion.72, bf16[2,2,96,640]{3,2,1,0:T(8,128)(2,1)S(1)} %collective-permute-done), kind=kLoop, calls=%fused_computation.6 | loop fusion | flops 14791680 | bytes 3938304 | tf_op jit(solution)/shard_map/concatenate | solution.py:22
  115.5 0.6 fusion.64
  116.1 0.7 fusion.62
  117.2 0.7 multiply_reduce_fusion.1
  117.9 0.9 fusion.80
  118.9 1.4 multiply_reduce_fusion
  120.4 3.8 %collective-permute-start.3 = (bf16[2,2,96,640]{3,2,1,0:T(8,128)(2,1)S(1)}, bf16[2,2,96,640]{3,2,1,0:T(8,128)(2,1)S(1)}, u32[]{:S(2)}, u32[]{:S(2)}) collective-permute-start(bf16[2,2,96,640]{3,2,1,0:T(8,128)(2,1)S(1)} %fusion.169), channel_id=1, source_target_pairs={{16,0},{32,16},{48,32},{64,48},{80,64},{96,80},{112,96},{128,112},... | collective-permute-start | bytes 1474568 | tf_op jit(solution)/shard_map/ppermute | solution.py:13
  124.2 0.4 fusion.183
  124.6 6.0 %collective-permute-done.3 = bf16[2,2,96,640]{3,2,1,0:T(8,128)(2,1)S(1)} collective-permute-done((bf16[2,2,96,640]{3,2,1,0:T(8,128)(2,1)S(1)}, bf16[2,2,96,640]{3,2,1,0:T(8,128)(2,1)S(1)}, u32[]{:S(2)}, u32[]{:S(2)}) %collective-permute-start.3) | collective-permute-done | bytes 491552 | tf_op jit(solution)/shard_map/ppermute | solution.py:13
  130.7 1.9 %collective-permute-start.5 = (bf16[4,1,96,640]{3,2,1,0:T(8,128)(2,1)S(1)}, bf16[4,1,96,640]{3,2,1,0:T(8,128)(2,1)S(1)}, u32[]{:S(2)}, u32[]{:S(2)}) collective-permute-start(bf16[4,1,96,640]{3,2,1,0:T(8,128)(2,1)S(1)} %get-tuple-element.6), channel_id=1, source_target_pairs={{1,0},{2,1},{3,2},{4,3},{5,4},{6,5},{7,6},{8,7},{9,8},{10,9},{11,1... | collective-permute-start | bytes 1474568 | tf_op jit(solution)/shard_map/ppermute | solution.py:26
  132.6 3.5 %collective-permute-start.4 = (bf16[4,1,96,640]{3,2,1,0:T(8,128)(2,1)S(1)}, bf16[4,1,96,640]{3,2,1,0:T(8,128)(2,1)S(1)}, u32[]{:S(2)}, u32[]{:S(2)}) collective-permute-start(bf16[4,1,96,640]{3,2,1,0:T(8,128)(2,1)S(1)} %get-tuple-element.5), channel_id=1, source_target_pairs={{0,1},{1,2},{2,3},{3,4},{4,5},{5,6},{6,7},{7,8},{8,9},{9,10},{10,1... | collective-permute-start | bytes 1474568 | tf_op jit(solution)/shard_map/ppermute | solution.py:24
  136.2 0.4 fusion.68
  136.9 8.6 %collective-permute-done.5 = bf16[4,1,96,640]{3,2,1,0:T(8,128)(2,1)S(1)} collective-permute-done((bf16[4,1,96,640]{3,2,1,0:T(8,128)(2,1)S(1)}, bf16[4,1,96,640]{3,2,1,0:T(8,128)(2,1)S(1)}, u32[]{:S(2)}, u32[]{:S(2)}) %collective-permute-start.5) | collective-permute-done | bytes 491552 | tf_op jit(solution)/shard_map/ppermute | solution.py:26
  145.5 4.0 %collective-permute-done.4 = bf16[4,1,96,640]{3,2,1,0:T(8,128)(2,1)S(1)} collective-permute-done((bf16[4,1,96,640]{3,2,1,0:T(8,128)(2,1)S(1)}, bf16[4,1,96,640]{3,2,1,0:T(8,128)(2,1)S(1)}, u32[]{:S(2)}, u32[]{:S(2)}) %collective-permute-start.4) | collective-permute-done | bytes 491552 | tf_op jit(solution)/shard_map/ppermute | solution.py:24
  149.5 1.8 %select_maximum_fusion = bf16[4,4,96,642]{3,2,1,0:T(8,128)(2,1)S(1)} fusion(bf16[4,1,96,640]{3,2,1,0:T(8,128)(2,1)S(1)} %collective-permute-done.5, bf16[4,1,96,640]{3,2,1,0:T(8,128)(2,1)S(1)} %collective-permute-done.4, bf16[2,2,96,640]{3,2,1,0:T(8,128)(2,1)S(1)} %collective-permute-done.3, bf16[2,2,96,640]{3,2,1,0:T(8,128)(2,1)S(1)} %fusion.169), kind=kLoop, calls=%fused_computation.3 | loop fusion | flops 14791680 | bytes 3938304 | tf_op jit(solution)/shard_map/concatenate | solution.py:22
  151.3 0.4 fusion.98
  151.8 0.4 fusion.100
  152.2 0.4 fusion.102
  152.6 0.4 fusion.104
  153.0 0.4 fusion.106
  153.8 0.4 fusion.111
  154.2 0.4 fusion.113
  154.6 0.4 fusion.115
  155.0 0.4 fusion.117
  155.4 0.4 fusion.88
  155.8 0.4 fusion.90
  156.3 0.4 fusion.93
  157.0 0.4 fusion.191
  157.4 0.5 fusion.40
  158.3 0.4 fusion.211
  158.7 0.7 fusion.57
  159.4 0.4 fusion.218
  159.9 0.4 fusion.233
  160.3 0.7 fusion.55
  161.0 0.4 fusion.176
  161.7 1.0 fusion.74
  162.7 1.2 fusion.78
  (59 shorter events, 10.9 us)
Async XLA Ops:
  0.0 117.9 %copy-start = (f32[3,96]{1,0:T(4,128)S(1)}, f32[3,96]{1,0:T(4,128)}, u32[]{:S(2)}) copy-start(f32[3,96]{1,0:T(4,128)} %param.12) | copy-start | bytes 3460
  1.2 91.9 %copy-start.3 = (bf16[96,2592]{1,0:T(8,128)(2,1)S(1)}, bf16[96,2592]{1,0:T(8,128)(2,1)}, u32[]{:S(2)}) copy-start(bf16[96,2592]{1,0:T(8,128)(2,1)} %param.10) | copy-start | bytes 1492996
  2.7 85.0 %collective-permute-start = (bf16[2,2,96,640]{3,2,1,0:T(8,128)(2,1)S(1)}, bf16[2,2,96,640]{3,2,1,0:T(8,128)(2,1)S(1)}, u32[]{:S(2)}, u32[]{:S(2)}) collective-permute-start(bf16[2,2,96,640]{3,2,1,0:T(8,128)(2,1)S(1)} %fusion.72), channel_id=1, source_target_pairs={{0,16},{16,32},{32,48},{48,64},{64,80},{80,96},{96,112},{112,128},... | collective-permute-start | bytes 1474568 | tf_op jit(solution)/shard_map/ppermute | solution.py:13
  87.8 14.0 %collective-permute-start.2 = (bf16[4,1,96,640]{3,2,1,0:T(8,128)(2,1)S(1)}, bf16[4,1,96,640]{3,2,1,0:T(8,128)(2,1)S(1)}, u32[]{:S(2)}, u32[]{:S(2)}) collective-permute-start(bf16[4,1,96,640]{3,2,1,0:T(8,128)(2,1)S(1)} %get-tuple-element.10), channel_id=1, source_target_pairs={{1,0},{2,1},{3,2},{4,3},{5,4},{6,5},{7,6},{8,7},{9,8},{10,9},{11,1... | collective-permute-start | bytes 1474568 | tf_op jit(solution)/shard_map/ppermute | solution.py:26
  90.3 15.8 %collective-permute-start.1 = (bf16[4,1,96,640]{3,2,1,0:T(8,128)(2,1)S(1)}, bf16[4,1,96,640]{3,2,1,0:T(8,128)(2,1)S(1)}, u32[]{:S(2)}, u32[]{:S(2)}) collective-permute-start(bf16[4,1,96,640]{3,2,1,0:T(8,128)(2,1)S(1)} %get-tuple-element.9), channel_id=1, source_target_pairs={{0,1},{1,2},{2,3},{3,4},{4,5},{5,6},{6,7},{7,8},{8,9},{9,10},{10,1... | collective-permute-start | bytes 1474568 | tf_op jit(solution)/shard_map/ppermute | solution.py:24
  116.1 1.0 copy-start.2
  117.2 0.8 copy-start.7
  117.9 1.0 copy-start.4
  117.9 1.0 copy-start.5
  120.4 10.1 %collective-permute-start.3 = (bf16[2,2,96,640]{3,2,1,0:T(8,128)(2,1)S(1)}, bf16[2,2,96,640]{3,2,1,0:T(8,128)(2,1)S(1)}, u32[]{:S(2)}, u32[]{:S(2)}) collective-permute-start(bf16[2,2,96,640]{3,2,1,0:T(8,128)(2,1)S(1)} %fusion.169), channel_id=1, source_target_pairs={{16,0},{32,16},{48,32},{64,48},{80,64},{96,80},{112,96},{128,112},... | collective-permute-start | bytes 1474568 | tf_op jit(solution)/shard_map/ppermute | solution.py:13
  130.7 14.8 %collective-permute-start.5 = (bf16[4,1,96,640]{3,2,1,0:T(8,128)(2,1)S(1)}, bf16[4,1,96,640]{3,2,1,0:T(8,128)(2,1)S(1)}, u32[]{:S(2)}, u32[]{:S(2)}) collective-permute-start(bf16[4,1,96,640]{3,2,1,0:T(8,128)(2,1)S(1)} %get-tuple-element.6), channel_id=1, source_target_pairs={{1,0},{2,1},{3,2},{4,3},{5,4},{6,5},{7,6},{8,7},{9,8},{10,9},{11,1... | collective-permute-start | bytes 1474568 | tf_op jit(solution)/shard_map/ppermute | solution.py:26
  132.6 16.9 %collective-permute-start.4 = (bf16[4,1,96,640]{3,2,1,0:T(8,128)(2,1)S(1)}, bf16[4,1,96,640]{3,2,1,0:T(8,128)(2,1)S(1)}, u32[]{:S(2)}, u32[]{:S(2)}) collective-permute-start(bf16[4,1,96,640]{3,2,1,0:T(8,128)(2,1)S(1)} %get-tuple-element.5), channel_id=1, source_target_pairs={{0,1},{1,2},{2,3},{3,4},{4,5},{5,6},{6,7},{7,8},{8,9},{9,10},{10,1... | collective-permute-start | bytes 1474568 | tf_op jit(solution)/shard_map/ppermute | solution.py:24
  161.0 0.7 copy-start.6
  161.7 2.2 %copy-start.1 = (f32[3,96]{1,0:T(4,128)S(1)}, f32[3,96]{1,0:T(4,128)}, u32[]{:S(2)}) copy-start(f32[3,96]{1,0:T(4,128)} %param.12) | copy-start | bytes 3460
where the time goes:
time: 166 us; the launch traced here: 164 us
  blocking collectives  76.5 us (46%)
  waiting for transfers between devices  30.9 us (19%)
  matrix products  25.4 us (15%)
  starting transfers between devices  18.6 us (11%)
  other arithmetic  10.4 us (6%)
    psum x1, blocking collectives, local(): weight_sum = lax.psum(jnp.sum(pix_weight), ('tm', 'rows'))  76.5 us
    ppermute x2, waiting for transfers between devices, extended(): lax.ppermute(head, axis, [((i + 1) % count, i) for i in range(ends)])  16.6 us
    dot_general x27, matrix products, local(): jnp.einsum('oc,frow->frcw', w_tap, piece, preferred_element_type=jnp.floa...  12.1 us
    dot_general x27, matrix products, local(): jnp.einsum('oc,frcw->frow', w_tap, piece, preferred_element_type=jnp.floa...  11 us
    ppermute x2, waiting for transfers between devices, extended(): lax.ppermute(tail, axis, [(i, (i + 1) % count) for i in range(ends)])  8.39 us
    ppermute x2, starting transfers between devices, from_behind(): return lax.ppermute(block, axis, route)  7.88 us
    ppermute x2, starting transfers between devices, extended(): lax.ppermute(tail, axis, [(i, (i + 1) % count) for i in range(ends)])  6.28 us
    ppermute x2, waiting for transfers between devices, from_behind(): return lax.ppermute(block, axis, route)  5.96 us
  transfers between devices with their start and end apart: 6, of which 5 were waited for; matrix products, arithmetic and copies ran while one was open for 3% of the time, Pallas kernels for 0%

commit v1 on v0

v1 whole, which is shorter than its diff:
```python
import functools

import jax
import jax.numpy as jnp
from jax import lax
from jax.experimental import pallas as pl
from jax.experimental.pallas import tpu as pltpu
from jax.sharding import PartitionSpec as P

EPS = 1e-06
DELTA = 1.0
MESH = pl.DeviceIdType.MESH
F32 = jnp.float32
BF16 = jnp.bfloat16
L = 128
Z, UP, DOWN, TOP, BOT = range(5)
XT, XB = 5, 6


def kernel(
    n_tm, n_rows, n_x, n_chunks, chans,
    feats_hbm, gain_ref, w_hbm, og_ref, rgbw_ref, target_hbm, pix_hbm, seg_ref,
    out_hbm,
    fe, tgt, pix, wn, stack, wf, wb, prm, act, grad, dterm, rstd, gy, part, edge, obuf, wsum,
    lsem, osem, ssem, rsem, wssem, wrsem,
):
    t = lax.axis_index("tm")
    r = lax.axis_index("rows")
    tn, tp = lax.rem(t + 1, n_tm), lax.rem(t + n_tm - 1, n_tm)
    rn, rp = lax.rem(r + 1, n_rows), lax.rem(r + n_rows - 1, n_rows)
    n_y = n_rows // n_x
    x, y = lax.rem(r, n_x), r // n_x
    tl, th = lax.rem(t, 4), t // 4

    rounds = [
        [(t, y * n_x + lax.rem(x + k, n_x)) for k in range(1, n_x)],
        [(t, lax.rem(y + k, n_y) * n_x + x) for k in range(1, n_y)],
        [(th * 4 + lax.rem(tl + k, 4), r) for k in range(1, 4)],
        [(lax.rem(th + k, n_tm // 4) * 4 + tl, r) for k in range(1, n_tm // 4)],
    ]
    near = [(tn, r), (tp, r), (t, rn), (t, rp)]
    everyone = near + [d for group in rounds for d in group]
    bar = pltpu.get_barrier_semaphore()
    for d in everyone:
        pl.semaphore_signal(bar, inc=1, device_id=d, device_id_type=MESH)

    loads = [
        pltpu.make_async_copy(feats_hbm, fe, lsem.at[0]),
        pltpu.make_async_copy(pix_hbm, pix, lsem.at[1]),
        pltpu.make_async_copy(target_hbm, tgt, lsem.at[2]),
        pltpu.make_async_copy(w_hbm, wn, lsem.at[3]),
    ]
    for c in loads:
        c.start()

    for q, row in enumerate((gain_ref[...].reshape(1, chans), og_ref[...].reshape(1, chans), rgbw_ref[0:1, :], rgbw_ref[1:2, :], rgbw_ref[2:3, :])):
        prm[q] = jnp.broadcast_to(row, (L, chans)).T

    loads[1].wait()
    acc = jnp.zeros((1, L), F32)
    for f in range(2):
        for h in range(2):
            for k in range(n_chunks):
                acc = acc + jnp.sum(pix[f, h, :, k * L : (k + 1) * L], axis=0, keepdims=True)
    wsum[0, 0] = jnp.broadcast_to(acc, (8, L))

    loads[0].wait()
    for k in range(n_chunks):
        for f in range(2):
            for h in range(2):
                xf = fe[f, h, :, k * L : (k + 1) * L].astype(F32)
                rs = lax.rsqrt(jnp.mean(xf * xf, axis=0, keepdims=True) + EPS)
                xn = xf * rs * prm[0]
                sg = jax.nn.sigmoid(xn)
                act[k, 2 + f, 1 + h] = (xn * sg).astype(BF16)
                dterm[k, f, h] = sg * (1.0 + xn * (1.0 - sg)) * prm[0]
                rstd[k, f, h] = jnp.broadcast_to(rs, (8, L))

    pl.semaphore_wait(bar, len(everyone))

    even = lax.rem(t, 2) == 0
    odd = lax.rem(t, 2) == 1

    def remote(src, dst, ss, rs_, dev):
        return pltpu.make_async_remote_copy(
            src_ref=src, dst_ref=dst, send_sem=ss, recv_sem=rs_, device_id=dev, device_id_type=MESH
        )

    def copy(p, k, name):
        buf = act if p == 0 else grad
        own, oth = (pl.ds(2, 2), pl.ds(0, 2)) if p == 0 else (pl.ds(0, 2), pl.ds(2, 2))
        ahead = (tn, r) if p == 0 else (tp, r)
        up, down = (t, rp), (t, rn)
        src, dst, s, v, dev = dict(
            z=((own, pl.ds(1, 2)), (oth, pl.ds(1, 2)), Z, Z, ahead),
            up=((own, 1), (own, 3), UP, UP, up),
            down=((own, 2), (own, 0), DOWN, DOWN, down),
            xup=((oth, 1), (oth, 3), XB, BOT, up),
            xdown=((oth, 2), (oth, 0), XT, TOP, down),
            ttop=((own, 0), (oth, 0), TOP, TOP, ahead),
            tbot=((own, 3), (oth, 3), BOT, BOT, ahead),
        )[name]
        return remote(buf.at[(k, *src)], buf.at[(k, *dst)], ssem.at[p, k, s], rsem.at[p, k, v], dev)

    relays = (even, odd)

    def send(p, k):
        copy(p, k, "up").start()
        copy(p, k, "down").start()
        copy(p, k, "z").start()

    def relay_z(p, k):
        copy(p, k, "z").wait_recv()

        @pl.when(relays[p])
        def _():
            copy(p, k, "xup").start()
            copy(p, k, "xdown").start()

    def relay_rows(p, k):
        copy(p, k, "up").wait_recv()
        copy(p, k, "down").wait_recv()

        @pl.when(relays[p])
        def _():
            copy(p, k, "ttop").start()
            copy(p, k, "tbot").start()

    def corners(p, k):
        copy(p, k, "ttop").wait_recv()
        copy(p, k, "tbot").wait_recv()

    def sum_copies(q):
        return [
            remote(wsum.at[q, 0], wsum.at[q, k + 1], wssem.at[q, k], wrsem.at[q, k], d)
            for k, d in enumerate(rounds[q])
        ]

    def sum_start(q):
        for c in sum_copies(q):
            c.start()

    def sum_end(q):
        cs = sum_copies(q)
        for c in cs:
            c.wait_recv()
        wsum[q + 1, 0] = sum(wsum[q, k + 1] for k in range(len(cs))) + wsum[q, 0]

    for k in range(n_chunks):
        send(0, k)
    sum_start(0)

    loads[3].wait()
    kdim = 9 * chans
    lane = lax.broadcasted_iota(jnp.int32, (1, kdim), 1)
    first = [(lane >= a * 3 * chans) & (lane < a * 3 * chans + chans) for a in range(3)]
    last = [(lane >= (a * 3 + 2) * chans) & (lane < (a * 3 + 3) * chans) for a in range(3)]
    any_first = (first[0] | first[1]) | first[2]
    any_last = (last[0] | last[1]) | last[2]
    has_top = jnp.where(r > 0, 1.0, 0.0).astype(F32)
    has_bot = jnp.where(r < n_rows - 1, 1.0, 0.0).astype(F32)
    frames = 2 * n_tm
    seg = [seg_ref[lax.rem(2 * t + frames - 2 + q, frames)] for q in range(6)]
    has_before = jnp.where(t > 0, 1.0, 0.0).astype(F32)
    has_after = jnp.where(t < n_tm - 1, 1.0, 0.0).astype(F32)

    def same(a, b):
        return jnp.where(seg[a] == seg[b], 1.0, 0.0).astype(F32)

    def masks(near_, far_, backward):
        made = []
        for f in range(2):
            lo, mid, hi = (1.0, near_[f], far_[f]) if backward else (far_[f], near_[f], 1.0)
            byframe = jnp.where(lane < 3 * chans, lo, jnp.where(lane < 6 * chans, mid, hi))
            made.append(byframe * jnp.where(any_first, has_top, 1.0))
            made.append(byframe * jnp.where(any_last, has_bot, 1.0))
        return made

    for l in range(3):
        for ij in range(9):
            q = ij * 3 + l
            stack[l * chans : (l + 1) * chans, ij * chans : (ij + 1) * chans] = wn[:, q * chans : (q + 1) * chans]
    fm = masks((same(1, 2) * has_before, same(2, 3)), (same(0, 2) * has_before, same(1, 3) * has_before), False)
    for q in range(4):
        wf[q] = stack[...] * fm[q].astype(BF16)

    eye = (
        lax.broadcasted_iota(jnp.int32, (chans, chans), 0) == lax.broadcasted_iota(jnp.int32, (chans, chans), 1)
    ).astype(BF16)
    bm = masks((same(2, 3), same(3, 4) * has_after), (same(2, 4) * has_after, same(3, 5) * has_after), True)
    for m in range(3):
        rows_ = jnp.concatenate(
            [wn[:, ((8 - ab) * 3 + 2 - m) * chans : ((8 - ab) * 3 + 3 - m) * chans] for ab in range(9)], axis=0
        )
        turned = lax.dot_general(eye, rows_, (((1,), (1,)), ((), ())), preferred_element_type=F32).astype(BF16)
        for q in range(4):
            wb[q, m * chans : (m + 1) * chans, :] = turned * bm[q].astype(BF16)

    col = lax.broadcasted_iota(jnp.int32, (chans, L), 1)

    def conv(weights, buf, k, f, h, base):
        prod = jnp.dot(weights[f * 2 + h], buf[k, f : f + 3, h : h + 3].reshape(kdim, L), preferred_element_type=F32)
        right = pltpu.roll(prod[:chans], 1, axis=1)
        left = pltpu.roll(prod[2 * chans :], L - 1, axis=1)
        done = None
        if k > 0:
            done = part[f, h] + jnp.where(col == L - 1, left, 0.0)
            right_in = edge[f, h]
        else:
            right_in = jnp.zeros((chans, L), F32)
        new = prod[chans : 2 * chans] + jnp.where(col == 0, right_in, right) + jnp.where(col == L - 1, 0.0, left)
        if base is not None:
            new = new + base
        part[f, h] = new
        edge[f, h] = right
        return done

    def xfloat(k, f, h):
        return fe[f, h, :, k * L : (k + 1) * L].astype(F32)

    def middle(k, f, h, yy):
        og = prm[1]
        ys = lax.rsqrt(jnp.mean(yy * yy, axis=0, keepdims=True) + EPS)
        yh = yy * ys
        yn = yh * og
        sg = jax.nn.sigmoid(yn)
        zz = yn * sg
        gz = jnp.zeros((chans, L), F32)
        for e in range(3):
            rgb = jnp.sum(prm[2 + e] * zz, axis=0, keepdims=True)
            d = jnp.clip(rgb - tgt[f, h, e : e + 1, k * L : (k + 1) * L], -DELTA, DELTA)
            gz = gz + prm[2 + e] * (pix[f, h, e : e + 1, k * L : (k + 1) * L] * d)
        v = gz * sg * (1.0 + yn * (1.0 - sg)) * og
        vp = jnp.mean(v * yh, axis=0, keepdims=True)
        g = ys * (v - yh * vp)
        gy[k, f, h] = g
        grad[k, f, 1 + h] = g.astype(BF16)

    def final(k, f, h, ga, scale):
        rs = rstd[k, f, h, 0:1, :]
        xh = xfloat(k, f, h) * rs
        u = ga * dterm[k, f, h]
        pj = jnp.mean(u * xh, axis=0, keepdims=True)
        res = (gy[k, f, h] + rs * (u - xh * pj)) * scale
        obuf[f, h, :, k * L : (k + 1) * L] = res.astype(BF16)

    def store(k):
        return pltpu.make_async_copy(
            obuf.at[:, :, :, pl.ds(k * L, L)], out_hbm.at[:, :, :, pl.ds(k * L, L)], osem.at[k]
        )

    cells = [(f, h) for f in range(2) for h in range(2)]
    loads[2].wait()

    ahead = 2
    for k in range(min(ahead, n_chunks)):
        relay_rows(0, k)
        relay_z(0, k)
    for k in range(n_chunks):
        if k + ahead < n_chunks:
            relay_rows(0, k + ahead)
            relay_z(0, k + ahead)
        corners(0, k)
        for f, h in cells:
            done = conv(wf, act, k, f, h, xfloat(k, f, h))
            if k > 0:
                middle(k - 1, f, h, done)
        if k > 0:
            send(1, k - 1)
        if k < 3:
            sum_end(k)
            sum_start(k + 1)
        if k >= 3:
            relay_rows(1, k - 3)
            relay_z(1, k - 3)
    for f, h in cells:
        middle(n_chunks - 1, f, h, part[f, h])
    send(1, n_chunks - 1)
    sum_end(3)
    total = jnp.sum(wsum[4, 0, 0:1, :], axis=1, keepdims=True)
    scale = jnp.full((1, 1), 2.0 * n_tm * 2.0 * n_rows * 3.0 * n_chunks * L, F32) / total

    relayed = max(n_chunks - 3, 0)
    for k in range(n_chunks):
        while relayed < min(k + ahead + 1, n_chunks):
            relay_rows(1, relayed)
            relay_z(1, relayed)
            relayed += 1
        corners(1, k)
        for f, h in cells:
            done = conv(wb, grad, k, f, h, None)
            if k > 0:
                final(k - 1, f, h, done, scale)
        if k > 0:
            store(k - 1).start()
    for f, h in cells:
        final(n_chunks - 1, f, h, part[f, h], scale)
    store(n_chunks - 1).start()

    for p in range(2):
        for k in range(n_chunks):
            for name in ("up", "down", "z"):
                copy(p, k, name).wait_send()

            @pl.when(relays[p])
            def _():
                for name in ("xup", "xdown", "ttop", "tbot"):
                    copy(p, k, name).wait_send()

    for q in range(4):
        for c in sum_copies(q):
            c.wait_send()
    for k in range(n_chunks):
        store(k).wait()


def local(feats, gain, conv_weight, out_gain, rgb_weight, target, pix_weight, frame_seg):
    n_tm, n_rows = lax.axis_size("tm"), lax.axis_size("rows")
    frames, rows, chans, width = feats.shape
    nc = width // L
    hbm = pl.BlockSpec(memory_space=pl.ANY)
    vmem = pl.BlockSpec(memory_space=pltpu.VMEM)
    smem = pl.BlockSpec(memory_space=pltpu.SMEM)
    kd = 9 * chans
    return pl.pallas_call(
        functools.partial(kernel, n_tm, n_rows, 4, nc, chans),
        out_shape=jax.ShapeDtypeStruct(feats.shape, BF16),
        in_specs=[hbm, vmem, hbm, vmem, vmem, hbm, hbm, smem],
        out_specs=hbm,
        scratch_shapes=[
            pltpu.VMEM(feats.shape, BF16),
            pltpu.VMEM(target.shape, F32),
            pltpu.VMEM(pix_weight.shape, F32),
            pltpu.VMEM(conv_weight.shape, BF16),
            pltpu.VMEM((3 * chans, kd), BF16),
            pltpu.VMEM((4, 3 * chans, kd), BF16),
            pltpu.VMEM((4, 3 * chans, kd), BF16),
            pltpu.VMEM((5, chans, L), F32),
            pltpu.VMEM((nc, 4, 4, chans, L), BF16),
            pltpu.VMEM((nc, 4, 4, chans, L), BF16),
            pltpu.VMEM((nc, 2, 2, chans, L), F32),
            pltpu.VMEM((nc, 2, 2, 8, L), F32),
            pltpu.VMEM((nc, 2, 2, chans, L), F32),
            pltpu.VMEM((2, 2, chans, L), F32),
            pltpu.VMEM((2, 2, chans, L), F32),
            pltpu.VMEM(feats.shape, BF16),
            pltpu.VMEM((5, 4, 8, L), F32),
            pltpu.SemaphoreType.DMA((4,)),
            pltpu.SemaphoreType.DMA((nc,)),
            pltpu.SemaphoreType.DMA((2, nc, 7)),
            pltpu.SemaphoreType.DMA((2, nc, 5)),
            pltpu.SemaphoreType.DMA((4, 3)),
            pltpu.SemaphoreType.DMA((4, 3)),
        ],
        compiler_params=pltpu.CompilerParams(
            collective_id=0, has_side_effects=True, vmem_limit_bytes=56 * 1024 * 1024
        ),
    )(feats, gain, conv_weight, out_gain, rgb_weight, target, pix_weight, frame_seg)


def solution(mesh):
    placed = (
        P("tm", "rows", None, None),
        P(),
        P(),
        P(),
        P(),
        P("tm", "rows", None, None),
        P("tm", "rows", None, None),
        P(),
    )
    return jax.shard_map(
        local, mesh=mesh, in_specs=placed, out_specs=P("tm", "rows", None, None), check_vma=False
    )
```

time: 166 us -> 45.4 us (0.27)
  the two profiles are of different devices: /device:TPU:57 before, /device:TPU:1 now
where the time goes in v1:
time: 45.4 us; the launch traced here: 45.2 us
  Pallas kernels  41.3 us (91%)
  local copies, waits for them, and re-layouts  3.86 us (9%)
    pallas_call x1, Pallas kernels, local(): pl.pallas_call(functools.partial(kernel, n_tm, n_rows, 4, nc, chans), out...  41.3 us
    unnamed x5, local copies, waits for them, and re-layouts  3.86 us

profile of v1, /device:TPU:1, one launch (start us, length us, event | category | flops | bytes accessed | tf_op | source)
XLA Modules:
  0.0 45.2 jit_solution(4533846750370322524)
XLA Ops:
  0.0 0.0 copy-start
  0.0 1.4 %copy.9.target_hbm = f32[2,2,3,640]{3,2,1,0:T(4,128)} copy(f32[2,2,3,640]{3,1,2,0:T(2,128)} %param.13) | data formatting | bytes 61440 | tf_op args[5]
  1.4 0.0 copy-done
  1.4 0.6 %copy.10.pix_hbm = f32[2,2,3,640]{3,2,1,0:T(4,128)} copy(f32[2,2,3,640]{3,1,2,0:T(2,128)S(1)} %copy-done) | data formatting | bytes 61440 | tf_op args[6]
  2.0 41.3 %shard_map.82 = bf16[2,2,96,640]{3,2,1,0:T(8,128)(2,1)} custom-call(bf16[2,2,96,640]{3,2,1,0:T(8,128)(2,1)} %feats_hbm.1, f32[96]{0:T(128)} %gain_ref.1, bf16[96,2592]{1,0:T(8,128)(2,1)} %w_hbm.1, f32[96]{0:T(128)} %og_ref.1, f32[3,96]{1,0:T(4,128)} %rgbw_ref.1, f32[2,2,3,640]{3,2,1,0:T(4,128)} %copy.9.target_hbm, f32[2,2,3,640]{3,2,1,0:T(4,128)} %copy.10.pix_hbm, ...), custom_call_target="tpu_custom_call" | custom-call | tf_op jit(solution)/shard_map/pallas_call | solution.py:325
  43.3 1.9 %copy.12 = bf16[2,2,96,640]{3,2,1,0:T(8,128)(2,1)} copy(bf16[2,2,96,640]{3,2,1,0:T(8,128)(2,1)} %shard_map.82) | data formatting | bytes 983040
Async XLA Ops:
  0.0 1.4 %copy-start = (f32[2,2,3,640]{3,1,2,0:T(2,128)S(1)}, f32[2,2,3,640]{3,1,2,0:T(2,128)}, u32[]{:S(2)}) copy-start(f32[2,2,3,640]{3,1,2,0:T(2,128)} %param.14) | copy-start | bytes 92164

commit v2 on v1

v2 whole, which is shorter than its diff:
```python
import functools

import jax
import jax.numpy as jnp
from jax import lax
from jax.experimental import pallas as pl
from jax.experimental.pallas import tpu as pltpu
from jax.sharding import PartitionSpec as P

EPS = 1e-06
DELTA = 1.0
MESH = pl.DeviceIdType.MESH
F32 = jnp.float32
BF16 = jnp.bfloat16
L = 128
Z, UP, DOWN = range(3)

def kernel(
    n_tm, n_rows, n_x, n_chunks, chans,
    feats_hbm, gain_ref, w_hbm, og_ref, rgbw_ref, target_hbm, pix_hbm, seg_ref,
    out_hbm,
    fe, tgt, pix, wn, mid_raw, out_raw, w_mid, w_out, prm, act, grad, dterm, rstd, gy, acc, part, edge, give, take, obuf, wsum, zsum,
    lsem, osem, ssem, rsem, wssem, wrsem, zssem, zrsem, hsem,
):
    t = lax.axis_index("tm")
    r = lax.axis_index("rows")
    n_y = n_rows // n_x
    x, y = lax.rem(r, n_x), r // n_x
    n_z = n_tm // 2
    not_first, not_last = t > 0, t < n_tm - 1
    has_up, has_down = r > 0, r < n_rows - 1

    group_x = [(t, y * n_x + lax.rem(x + k, n_x)) for k in range(1, n_x)]
    group_y = [(t, lax.rem(y + k, n_y) * n_x + x) for k in range(1, n_y)]
    mate = (t + 1 - 2 * lax.rem(t, 2), r)
    rounds = [group_x, group_y, [mate]]

    def along(d):
        return (t + 2 * d, r), (t + 2 * d >= 0 if d < 0 else t + 2 * d < n_tm)

    greet = [((t + 1, r), not_last), ((t - 1, r), not_first), ((t, r + 1), has_down), ((t, r - 1), has_up)]
    greet += [along(1), along(-1)] + [(d, None) for d in group_x + group_y]
    bar = pltpu.get_barrier_semaphore()

    def signal(sem, partners):
        for d, there in partners:
            if there is None:
                pl.semaphore_signal(sem, inc=1, device_id=d, device_id_type=MESH)
            else:

                @pl.when(there)
                def _():
                    pl.semaphore_signal(sem, inc=1, device_id=d, device_id_type=MESH)

    def await_all(sem, partners):
        amount = sum(1 if there is None else jnp.where(there, 1, 0) for _, there in partners)
        pl.semaphore_wait(sem, amount)

    signal(bar, greet)

    loads = [
        pltpu.make_async_copy(feats_hbm, fe, lsem.at[0]),
        pltpu.make_async_copy(pix_hbm, pix, lsem.at[1]),
        pltpu.make_async_copy(w_hbm, wn, lsem.at[3]),
        pltpu.make_async_copy(target_hbm, tgt, lsem.at[2]),
    ]
    for c in loads:
        c.start()

    @pl.when(jnp.logical_not(has_up))
    def _():
        take[:, :, 0] = jnp.zeros((2, n_chunks, 2, chans, L), BF16)

    @pl.when(jnp.logical_not(has_down))
    def _():
        take[:, :, 1] = jnp.zeros((2, n_chunks, 2, chans, L), BF16)

    @pl.when(jnp.logical_not(not_first))
    def _():
        act[:, 0:2] = jnp.zeros((n_chunks, 2, 2, chans, L), BF16)

    @pl.when(jnp.logical_not(not_last))
    def _():
        grad[:, 2:4] = jnp.zeros((n_chunks, 2, 2, chans, L), BF16)

    def column(row):
        return jnp.broadcast_to(row, (L, chans)).T

    prm[0] = column(gain_ref[...].reshape(1, chans))

    def remote(src, dst, ss, rs_, dev):
        return pltpu.make_async_remote_copy(
            src_ref=src, dst_ref=dst, send_sem=ss, recv_sem=rs_, device_id=dev, device_id_type=MESH
        )

    def copy(p, k, name):
        s, v = ssem.at[p, k], rsem.at[p, k]
        if name == Z:
            buf = (act if p == 0 else grad).at[k]
            own, oth = (pl.ds(2, 2), pl.ds(0, 2)) if p == 0 else (pl.ds(0, 2), pl.ds(2, 2))
            return remote(buf.at[own], buf.at[oth], s.at[Z], v.at[Z], (t + 1 - 2 * p, r))
        if name == UP:
            return remote(give.at[p, k, 0], take.at[p, k, 1], s.at[UP], v.at[UP], (t, r - 1))
        return remote(give.at[p, k, 1], take.at[p, k, 0], s.at[DOWN], v.at[DOWN], (t, r + 1))

    leaves = ({Z: not_last, UP: has_up, DOWN: has_down}, {Z: not_first, UP: has_up, DOWN: has_down})
    comes = ({Z: not_first, UP: has_down, DOWN: has_up}, {Z: not_last, UP: has_down, DOWN: has_up})

    def send(p, k, *names):
        for name in names:

            @pl.when(leaves[p][name])
            def _():
                copy(p, k, name).start()

    def receive(p, k, *names):
        for name in names:

            @pl.when(comes[p][name])
            def _():
                copy(p, k, name).wait_recv()

    def sum_copies(q):
        return [
            remote(wsum.at[q, 0], wsum.at[q, k + 1], wssem.at[q, k], wrsem.at[q, k], d)
            for k, d in enumerate(rounds[q])
        ]

    def sum_start(q):
        for c in sum_copies(q):
            c.start()

    def sum_end(q):
        cs = sum_copies(q)
        for c in cs:
            c.wait_recv()
        wsum[q + 1, 0] = sum(wsum[q, k + 1] for k in range(len(cs))) + wsum[q, 0]

    reach = [d for d in range(1 - n_z, n_z) if d != 0]

    def chip_copy(d):
        return remote(zsum.at[n_z - 1], zsum.at[n_z - 1 + d], zssem.at[n_z - 1 + d], zrsem.at[n_z - 1 + d], along(d)[0])

    def chips_start():
        zsum[n_z - 1] = wsum[3, 0]
        for d in reach:

            @pl.when(along(d)[1])
            def _():
                chip_copy(d).start()

    def chips_end():
        for d in reach:

            @pl.when(along(-d)[1])
            def _():
                chip_copy(d).wait_recv()

        everything = sum(zsum[q, 0:1, :] for q in range(2 * n_z - 1))
        total = jnp.sum(everything, axis=1, keepdims=True)
        return jnp.full((1, 1), 2.0 * n_tm * 2.0 * n_rows * 3.0 * n_chunks * L, F32) / total

    chain = [[along(1), along(-1)], [along(2), along(-2)], [along(4), along(-4)]]

    def hail(q):
        signal(hsem.at[q], chain[q])

    def hailed(q):
        await_all(hsem.at[q], chain[q])

    loads[0].wait()
    for k in range(n_chunks):
        for f in range(2):
            for h in range(2):
                xf = fe[f, h, :, k * L : (k + 1) * L].astype(F32)
                rs = lax.rsqrt(jnp.mean(xf * xf, axis=0, keepdims=True) + EPS)
                xn = xf * rs * prm[0]
                sg = jax.nn.sigmoid(xn)
                act[k, 2 + f, h] = (xn * sg).astype(BF16)
                dterm[k, f, h] = sg * (1.0 + xn * (1.0 - sg)) * prm[0]
                rstd[k, f, h] = jnp.broadcast_to(rs, (8, L))
        if k == 0:
            await_all(bar, greet)
        send(0, k, Z)

    loads[1].wait()
    weight = jnp.zeros((1, L), F32)
    for f in range(2):
        for e in range(3):
            for k in range(n_chunks):
                weight = weight + jnp.sum(pix[f, e, :, k * L : (k + 1) * L], axis=0, keepdims=True)
    wsum[0, 0] = jnp.broadcast_to(weight, (8, L))
    zsum[...] = jnp.zeros_like(zsum)
    sum_start(0)
    hail(0)
    for q, row in enumerate((og_ref[...].reshape(1, chans), rgbw_ref[0:1, :], rgbw_ref[1:2, :], rgbw_ref[2:3, :])):
        prm[1 + q] = column(row)

    loads[2].wait()
    tall = 3 * chans
    frames = 2 * n_tm
    seg = [seg_ref[lax.rem(2 * t + frames - 2 + q, frames)] for q in range(6)]

    def same(a, b):
        return jnp.where(seg[a] == seg[b], 1.0, 0.0).astype(F32)

    def mask(near_, far_, backward, rows_):
        lane = lax.broadcasted_iota(jnp.int32, (1, 3 * rows_ * chans), 1)
        lo, mid, hi = (1.0, near_, far_) if backward else (far_, near_, 1.0)
        return jnp.where(lane < rows_ * chans, lo, jnp.where(lane < 2 * rows_ * chans, mid, hi)).astype(BF16)

    def tap(q):
        return wn[:, q * chans : (q + 1) * chans]

    eye = (
        lax.broadcasted_iota(jnp.int32, (chans, chans), 0) == lax.broadcasted_iota(jnp.int32, (chans, chans), 1)
    ).astype(BF16)

    inner = [(0, (0, 1)), (1, (0, 1))]
    outer = [(-1, (0,)), (2, (1,))]

    def prepare(p):
        for part_of, raw, made in ((inner, mid_raw, w_mid), (outer, out_raw, w_out)):
            for n, (to, sources) in enumerate(part_of):
                for l in range(3):
                    at = n * tall + l * chans
                    if p == 0:
                        taps = [tap((i * 3 + h - to + 1) * 3 + l) for i in range(3) for h in sources]
                        for q, block in enumerate(taps):
                            raw[at : at + chans, q * chans : (q + 1) * chans] = block
                    else:
                        taps = [tap(((2 - a) * 3 + to + 1 - h) * 3 + 2 - l) for a in range(3) for h in sources]
                        raw[at : at + chans, :] = lax.dot_general(
                            eye, jnp.concatenate(taps, axis=0), (((1,), (1,)), ((), ())), preferred_element_type=F32
                        ).astype(BF16)
            for f in range(2):
                near_, far_ = (same(1 + f, 2 + f), same(f, 2 + f)) if p == 0 else (same(2 + f, 3 + f), same(2 + f, 4 + f))
                made[p, f] = raw[...] * mask(near_, far_, p == 1, len(part_of[0][1]))

    prepare(0)
    col = lax.broadcasted_iota(jnp.int32, (chans, L), 1)

    def shifted(prod, k, f, row):
        right = pltpu.roll(prod[:chans], 1, axis=1)
        left = pltpu.roll(prod[2 * chans :], L - 1, axis=1)
        done = None
        right_in = jnp.zeros((chans, L), F32)
        if k > 0:
            done = part[f, row] + jnp.where(col == L - 1, left, 0.0)
            right_in = edge[f, row]
        new = prod[chans : 2 * chans] + jnp.where(col == 0, right_in, right) + jnp.where(col == L - 1, 0.0, left)
        if k < n_chunks - 1:
            part[f, row] = new
            edge[f, row] = right
        return done, new

    def conv(p, k):
        buf = act if p == 0 else grad
        for f in range(2):
            both = jnp.dot(w_mid[p, f], buf[k, f : f + 3].reshape(2 * tall, L), preferred_element_type=F32)
            above = jnp.dot(
                w_out[p, f, :tall], buf[k, f : f + 3, 0].reshape(tall, L), preferred_element_type=F32
            )
            below = jnp.dot(
                w_out[p, f, tall:], buf[k, f : f + 3, 1].reshape(tall, L), preferred_element_type=F32
            )
            for row, prod in enumerate((above, both[:tall], both[tall:], below)):
                for q, value in zip((k - 1, k), shifted(prod, k, f, row)):
                    if value is None or (q == k and k < n_chunks - 1):
                        continue
                    if row in (1, 2):
                        acc[q, f, row - 1] = value
                    else:
                        give[p, q, row // 3, f] = value.astype(BF16)
        if k > 0:
            send(p, k - 1, UP, DOWN)
        if k == n_chunks - 1:
            send(p, k, UP, DOWN)

    def xfloat(k, f, h):
        return fe[f, h, :, k * L : (k + 1) * L].astype(F32)

    def middle(k, f, h):
        yy = xfloat(k, f, h) + acc[k, f, h] + take[0, k, h, f].astype(F32)
        og = prm[1]
        ys = lax.rsqrt(jnp.mean(yy * yy, axis=0, keepdims=True) + EPS)
        yh = yy * ys
        yn = yh * og
        sg = jax.nn.sigmoid(yn)
        zz = yn * sg
        gz = jnp.zeros((chans, L), F32)
        for e in range(3):
            rgb = jnp.sum(prm[2 + e] * zz, axis=0, keepdims=True)
            d = jnp.clip(rgb - tgt[f, e, h : h + 1, k * L : (k + 1) * L], -DELTA, DELTA)
            gz = gz + prm[2 + e] * (pix[f, e, h : h + 1, k * L : (k + 1) * L] * d)
        v = gz * sg * (1.0 + yn * (1.0 - sg)) * og
        vp = jnp.mean(v * yh, axis=0, keepdims=True)
        g = ys * (v - yh * vp)
        gy[k, f, h] = g
        grad[k, f, h] = g.astype(BF16)

    def final(k, f, h, scale):
        ga = acc[k, f, h] + take[1, k, h, f].astype(F32)
        rs = rstd[k, f, h, 0:1, :]
        xh = xfloat(k, f, h) * rs
        u = ga * dterm[k, f, h]
        pj = jnp.mean(u * xh, axis=0, keepdims=True)
        res = (gy[k, f, h] + rs * (u - xh * pj)) * scale
        obuf[f, h, :, k * L : (k + 1) * L] = res.astype(BF16)

    def store(k):
        return pltpu.make_async_copy(
            obuf.at[:, :, :, pl.ds(k * L, L)], out_hbm.at[:, :, :, pl.ds(k * L, L)], osem.at[k]
        )

    cells = [(f, h) for f in range(2) for h in range(2)]
    loads[3].wait()

    sum_end(0)
    sum_start(1)
    for k in range(n_chunks):
        receive(0, k, Z)
        conv(0, k)
        if k == 1:
            sum_end(1)
            sum_start(2)
        if k == 2:
            hailed(0)
            hail(1)
    sum_end(2)
    hailed(1)
    hail(2)
    prepare(1)
    for k in range(n_chunks):
        receive(0, k, UP, DOWN)
        for f, h in cells:
            middle(k, f, h)
        send(1, k, Z)
    hailed(2)
    chips_start()

    for k in range(n_chunks):
        receive(1, k, Z)
        conv(1, k)
    scale = chips_end()
    for k in range(n_chunks):
        receive(1, k, UP, DOWN)
        for f, h in cells:
            final(k, f, h, scale)
        store(k).start()

    for p in range(2):
        for name, there in leaves[p].items():

            @pl.when(there)
            def _():
                for k in range(n_chunks):
                    copy(p, k, name).wait_send()

    for q in range(3):
        for c in sum_copies(q):
            c.wait_send()
    for d in reach:

        @pl.when(along(d)[1])
        def _():
            chip_copy(d).wait_send()

    for k in range(n_chunks):
        store(k).wait()


def local(feats, gain, conv_weight, out_gain, rgb_weight, target, pix_weight, frame_seg):
    n_tm, n_rows = lax.axis_size("tm"), lax.axis_size("rows")
    frames, rows, chans, width = feats.shape
    nc = width // L
    hbm = pl.BlockSpec(memory_space=pl.ANY)
    vmem = pl.BlockSpec(memory_space=pltpu.VMEM)
    smem = pl.BlockSpec(memory_space=pltpu.SMEM)
    tall = 3 * chans
    return pl.pallas_call(
        functools.partial(kernel, n_tm, n_rows, 4, nc, chans),
        out_shape=jax.ShapeDtypeStruct(feats.shape, BF16),
        in_specs=[hbm, vmem, hbm, vmem, vmem, hbm, hbm, smem],
        out_specs=hbm,
        scratch_shapes=[
            pltpu.VMEM(feats.shape, BF16),
            pltpu.VMEM((frames, 3, rows, width), F32),
            pltpu.VMEM((frames, 3, rows, width), F32),
            pltpu.VMEM(conv_weight.shape, BF16),
            pltpu.VMEM((2 * tall, 2 * tall), BF16),
            pltpu.VMEM((2 * tall, tall), BF16),
            pltpu.VMEM((2, 2, 2 * tall, 2 * tall), BF16),
            pltpu.VMEM((2, 2, 2 * tall, tall), BF16),
            pltpu.VMEM((5, chans, L), F32),
            pltpu.VMEM((nc, 4, 2, chans, L), BF16),
            pltpu.VMEM((nc, 4, 2, chans, L), BF16),
            pltpu.VMEM((nc, 2, 2, chans, L), F32),
            pltpu.VMEM((nc, 2, 2, 8, L), F32),
            pltpu.VMEM((nc, 2, 2, chans, L), F32),
            pltpu.VMEM((nc, 2, 2, chans, L), F32),
            pltpu.VMEM((2, 4, chans, L), F32),
            pltpu.VMEM((2, 4, chans, L), F32),
            pltpu.VMEM((2, nc, 2, 2, chans, L), BF16),
            pltpu.VMEM((2, nc, 2, 2, chans, L), BF16),
            pltpu.VMEM(feats.shape, BF16),
            pltpu.VMEM((4, 4, 8, L), F32),
            pltpu.VMEM((n_tm - 1, 8, L), F32),
            pltpu.SemaphoreType.DMA((4,)),
            pltpu.SemaphoreType.DMA((nc,)),
            pltpu.SemaphoreType.DMA((2, nc, 3)),
            pltpu.SemaphoreType.DMA((2, nc, 3)),
            pltpu.SemaphoreType.DMA((3, 3)),
            pltpu.SemaphoreType.DMA((3, 3)),
            pltpu.SemaphoreType.DMA((n_tm - 1,)),
            pltpu.SemaphoreType.DMA((n_tm - 1,)),
            pltpu.SemaphoreType.REGULAR((3,)),
        ],
        compiler_params=pltpu.CompilerParams(
            collective_id=0, has_side_effects=True, vmem_limit_bytes=56 * 1024 * 1024
        ),
    )(
        feats, gain, conv_weight, out_gain, rgb_weight,
        target.transpose(0, 2, 1, 3), pix_weight.transpose(0, 2, 1, 3), frame_seg,
    )


def solution(mesh):
    placed = (
        P("tm", "rows", None, None),
        P(),
        P(),
        P(),
        P(),
        P("tm", "rows", None, None),
        P("tm", "rows", None, None),
        P(),
    )
    return jax.shard_map(
        local, mesh=mesh, in_specs=placed, out_specs=P("tm", "rows", None, None), check_vma=False
    )
```

time: 45.4 us -> 36.7 us (0.81)
  Pallas kernels: 41.3 us -> 34.7 us
  local copies, waits for them, and re-layouts: 3.86 us -> 1.85 us
    pallas_call x1, Pallas kernels: 41.3 us -> 34.7 us  [local(): pl.pallas_call(functools.partial(kernel, n_tm, n_rows, 4, nc, chans), out...]
    unnamed x5 -> x1, local copies, waits for them, and re-layouts: 3.86 us -> 1.85 us
where the time goes in v2:
time: 36.7 us; the launch traced here: 36.5 us
  Pallas kernels  34.7 us (95%)
  local copies, waits for them, and re-layouts  1.85 us (5%)
    pallas_call x1, Pallas kernels, local(): pl.pallas_call(functools.partial(kernel, n_tm, n_rows, 4, nc, chans), out...  34.7 us
    unnamed x1, local copies, waits for them, and re-layouts  1.85 us

profile of v2, /device:TPU:1, one launch (start us, length us, event | category | flops | bytes accessed | tf_op | source)
XLA Modules:
  0.0 36.5 jit_solution(9116324978219782165)
XLA Ops:
  0.0 34.7 %shard_map.82 = bf16[2,2,96,640]{3,2,1,0:T(8,128)(2,1)} custom-call(bf16[2,2,96,640]{3,2,1,0:T(8,128)(2,1)} %feats_hbm.1, f32[96]{0:T(128)} %gain_ref.1, bf16[96,2592]{1,0:T(8,128)(2,1)} %w_hbm.1, f32[96]{0:T(128)} %og_ref.1, f32[3,96]{1,0:T(4,128)} %rgbw_ref.1, f32[2,3,2,640]{3,2,1,0:T(2,128)} %bitcast.2, f32[2,3,2,640]{3,2,1,0:T(2,128)} %bitcast.3, s32[32]{0:T(128)} %seg_ref.1), custom_call_target="tpu_custom_call" | custom-call | tf_op jit(solution)/shard_map/pallas_call | solution.py:381
  34.7 1.9 %copy.10 = bf16[2,2,96,640]{3,2,1,0:T(8,128)(2,1)} copy(bf16[2,2,96,640]{3,2,1,0:T(8,128)(2,1)} %shard_map.82) | data formatting | bytes 983040

commit v3 on v2

--- a/solution.py
+++ b/solution.py
@@ -17,23 +17,21 @@
 
 def kernel(
     n_tm, n_rows, n_x, n_chunks, chans,
-    feats_hbm, gain_ref, w_hbm, og_ref, rgbw_ref, target_hbm, pix_hbm, seg_ref,
+    feats_hbm, gain_hbm, w_hbm, og_hbm, rgbw_hbm, target_hbm, pix_hbm, seg_hbm,
     out_hbm,
-    fe, tgt, pix, wn, mid_raw, out_raw, w_mid, w_out, prm, act, grad, dterm, rstd, gy, acc, part, edge, give, take, obuf, wsum, zsum,
+    fe, gain_ref, og_ref, rgbw_ref, seg_ref, tgt, pix, wn, w_mid, w_out, rhs, prm, act, grad, dterm, rstd, gy, acc, part, edge, give, take, obuf, wsum, zsum,
     lsem, osem, ssem, rsem, wssem, wrsem, zssem, zrsem, hsem,
 ):
     t = lax.axis_index("tm")
     r = lax.axis_index("rows")
     n_y = n_rows // n_x
     x, y = lax.rem(r, n_x), r // n_x
-    n_z = n_tm // 2
     not_first, not_last = t > 0, t < n_tm - 1
     has_up, has_down = r > 0, r < n_rows - 1
 
     group_x = [(t, y * n_x + lax.rem(x + k, n_x)) for k in range(1, n_x)]
     group_y = [(t, lax.rem(y + k, n_y) * n_x + x) for k in range(1, n_y)]
-    mate = (t + 1 - 2 * lax.rem(t, 2), r)
-    rounds = [group_x, group_y, [mate]]
+    rounds = [group_x, group_y]
 
     def along(d):
         return (t + 2 * d, r), (t + 2 * d >= 0 if d < 0 else t + 2 * d < n_tm)
@@ -56,15 +54,23 @@
         amount = sum(1 if there is None else jnp.where(there, 1, 0) for _, there in partners)
         pl.semaphore_wait(sem, amount)
 
+    zsum[...] = jnp.zeros_like(zsum)
     signal(bar, greet)
 
-    loads = [
-        pltpu.make_async_copy(feats_hbm, fe, lsem.at[0]),
-        pltpu.make_async_copy(pix_hbm, pix, lsem.at[1]),
-        pltpu.make_async_copy(w_hbm, wn, lsem.at[3]),
-        pltpu.make_async_copy(target_hbm, tgt, lsem.at[2]),
-    ]
-    for c in loads:
+    loads = {
+        name: pltpu.make_async_copy(src, dst, lsem.at[q])
+        for q, (name, src, dst) in enumerate((
+            ("gain", gain_hbm, gain_ref),
+            ("feats", feats_hbm, fe),
+            ("pix", pix_hbm, pix),
+            ("seg", seg_hbm, seg_ref),
+            ("weights", w_hbm, wn),
+            ("out_gain", og_hbm, og_ref),
+            ("rgb", rgbw_hbm, rgbw_ref),
+            ("target", target_hbm, tgt),
+        ))
+    }
+    for c in loads.values():
         c.start()
 
     @pl.when(jnp.logical_not(has_up))
@@ -86,6 +92,7 @@
     def column(row):
         return jnp.broadcast_to(row, (L, chans)).T
 
+    loads["gain"].wait()
     prm[0] = column(gain_ref[...].reshape(1, chans))
 
     def remote(src, dst, ss, rs_, dev):
@@ -136,27 +143,31 @@
             c.wait_recv()
         wsum[q + 1, 0] = sum(wsum[q, k + 1] for k in range(len(cs))) + wsum[q, 0]
 
-    reach = [d for d in range(1 - n_z, n_z) if d != 0]
-
-    def chip_copy(d):
-        return remote(zsum.at[n_z - 1], zsum.at[n_z - 1 + d], zssem.at[n_z - 1 + d], zrsem.at[n_z - 1 + d], along(d)[0])
-
-    def chips_start():
-        zsum[n_z - 1] = wsum[3, 0]
+    reach = [d for d in range(1 - n_tm, n_tm) if d != 0]
+
+    def on_tm(d):
+        return t + d >= 0 if d < 0 else t + d < n_tm
+
+    def plane_copy(d):
+        q = n_tm - 1 + d
+        return remote(zsum.at[n_tm - 1], zsum.at[q], zssem.at[q], zrsem.at[q], (t + d, r))
+
+    def planes_start():
+        zsum[n_tm - 1] = wsum[2, 0]
         for d in reach:
 
-            @pl.when(along(d)[1])
+            @pl.when(on_tm(d))
             def _():
-                chip_copy(d).start()
-
-    def chips_end():
+                plane_copy(d).start()
+
+    def planes_end():
         for d in reach:
 
-            @pl.when(along(-d)[1])
+            @pl.when(on_tm(-d))
             def _():
-                chip_copy(d).wait_recv()
-
-        everything = sum(zsum[q, 0:1, :] for q in range(2 * n_z - 1))
+                plane_copy(d).wait_recv()
+
+        everything = sum(zsum[q, 0:1, :] for q in range(2 * n_tm - 1))
         total = jnp.sum(everything, axis=1, keepdims=True)
         return jnp.full((1, 1), 2.0 * n_tm * 2.0 * n_rows * 3.0 * n_chunks * L, F32) / total
 
@@ -168,7 +179,16 @@
     def hailed(q):
         await_all(hsem.at[q], chain[q])
 
-    loads[0].wait()
+    def weights_sum():
+        loads["pix"].wait()
+        weight = jnp.zeros((1, L), F32)
+        for f in range(2):
+            for e in range(3):
+                for k in range(n_chunks):
+                    weight = weight + jnp.sum(pix[f, e, :, k * L : (k + 1) * L], axis=0, keepdims=True)
+        wsum[0, 0] = jnp.broadcast_to(weight, (8, L))
+
+    loads["feats"].wait()
     for k in range(n_chunks):
         for f in range(2):
             for h in range(2):
@@ -182,21 +202,13 @@
         if k == 0:
             await_all(bar, greet)
         send(0, k, Z)
-
-    loads[1].wait()
-    weight = jnp.zeros((1, L), F32)
-    for f in range(2):
-        for e in range(3):
-            for k in range(n_chunks):
-                weight = weight + jnp.sum(pix[f, e, :, k * L : (k + 1) * L], axis=0, keepdims=True)
-    wsum[0, 0] = jnp.broadcast_to(weight, (8, L))
-    zsum[...] = jnp.zeros_like(zsum)
-    sum_start(0)
-    hail(0)
-    for q, row in enumerate((og_ref[...].reshape(1, chans), rgbw_ref[0:1, :], rgbw_ref[1:2, :], rgbw_ref[2:3, :])):
-        prm[1 + q] = column(row)
-
-    loads[2].wait()
+        if k == 0:
+            weights_sum()
+            sum_start(0)
+            hail(0)
+
+    loads["weights"].wait()
+    loads["seg"].wait()
     tall = 3 * chans
     frames = 2 * n_tm
     seg = [seg_ref[lax.rem(2 * t + frames - 2 + q, frames)] for q in range(6)]
@@ -204,10 +216,13 @@
     def same(a, b):
         return jnp.where(seg[a] == seg[b], 1.0, 0.0).astype(F32)
 
-    def mask(near_, far_, backward, rows_):
-        lane = lax.broadcasted_iota(jnp.int32, (1, 3 * rows_ * chans), 1)
-        lo, mid, hi = (1.0, near_, far_) if backward else (far_, near_, 1.0)
-        return jnp.where(lane < rows_ * chans, lo, jnp.where(lane < 2 * rows_ * chans, mid, hi)).astype(BF16)
+    def valid(p, f, i):
+        if i == (2 if p == 0 else 0):
+            return None
+        a, b = (f + i, f + 2) if p == 0 else (2 + f, 2 + f + i)
+        return jnp.full((1, L), same(a, b), F32).astype(BF16)
+
+    checks = [[[valid(p, f, i) for i in range(3)] for f in range(2)] for p in range(2)]
 
     def tap(q):
         return wn[:, q * chans : (q + 1) * chans]
@@ -220,7 +235,7 @@
     outer = [(-1, (0,)), (2, (1,))]
 
     def prepare(p):
-        for part_of, raw, made in ((inner, mid_raw, w_mid), (outer, out_raw, w_out)):
+        for part_of, raw in ((inner, w_mid.at[p]), (outer, w_out.at[p])):
             for n, (to, sources) in enumerate(part_of):
                 for l in range(3):
                     at = n * tall + l * chans
@@ -233,11 +248,12 @@
                         raw[at : at + chans, :] = lax.dot_general(
                             eye, jnp.concatenate(taps, axis=0), (((1,), (1,)), ((), ())), preferred_element_type=F32
                         ).astype(BF16)
-            for f in range(2):
-                near_, far_ = (same(1 + f, 2 + f), same(f, 2 + f)) if p == 0 else (same(2 + f, 3 + f), same(2 + f, 4 + f))
-                made[p, f] = raw[...] * mask(near_, far_, p == 1, len(part_of[0][1]))
 
     prepare(0)
+    for name in ("out_gain", "rgb", "target"):
+        loads[name].wait()
+    for q, row in enumerate((og_ref[...].reshape(1, chans), rgbw_ref[0:1, :], rgbw_ref[1:2, :], rgbw_ref[2:3, :])):
+        prm[1 + q] = column(row)
     col = lax.broadcasted_iota(jnp.int32, (chans, L), 1)
 
     def shifted(prod, k, f, row):
@@ -257,15 +273,17 @@
     def conv(p, k):
         buf = act if p == 0 else grad
         for f in range(2):
-            both = jnp.dot(w_mid[p, f], buf[k, f : f + 3].reshape(2 * tall, L), preferred_element_type=F32)
-            above = jnp.dot(
-                w_out[p, f, :tall], buf[k, f : f + 3, 0].reshape(tall, L), preferred_element_type=F32
-            )
-            below = jnp.dot(
-                w_out[p, f, tall:], buf[k, f : f + 3, 1].reshape(tall, L), preferred_element_type=F32
-            )
-            for row, prod in enumerate((above, both[:tall], both[tall:], below)):
-                for q, value in zip((k - 1, k), shifted(prod, k, f, row)):
+            for i in range(3):
+                block = buf[k, f + i]
+                if checks[p][f][i] is not None:
+                    block = block * checks[p][f][i]
+                rhs[k, i, :, :, f * L : (f + 1) * L] = block
+        both = jnp.dot(w_mid[p], rhs[k].reshape(2 * tall, 2 * L), preferred_element_type=F32)
+        above = jnp.dot(w_out[p, :tall], rhs[k, :, 0].reshape(tall, 2 * L), preferred_element_type=F32)
+        below = jnp.dot(w_out[p, tall:], rhs[k, :, 1].reshape(tall, 2 * L), preferred_element_type=F32)
+        for row, prod in enumerate((above, both[:tall], both[tall:], below)):
+            for f in range(2):
+                for q, value in zip((k - 1, k), shifted(prod[:, f * L : (f + 1) * L], k, f, row)):
                     if value is None or (q == k and k < n_chunks - 1):
                         continue
                     if row in (1, 2):
@@ -314,35 +332,41 @@
         )
 
     cells = [(f, h) for f in range(2) for h in range(2)]
-    loads[3].wait()
-
-    sum_end(0)
-    sum_start(1)
+
     for k in range(n_chunks):
         receive(0, k, Z)
         conv(0, k)
-        if k == 1:
-            sum_end(1)
-            sum_start(2)
+        if k in (1, 3):
+            hailed(k // 2)
+            hail(k // 2 + 1)
         if k == 2:
-            hailed(0)
-            hail(1)
-    sum_end(2)
-    hailed(1)
-    hail(2)
+            sum_end(0)
+            sum_start(1)
+    sum_end(1)
+
+    late = t >= n_tm // 2
+
+    @pl.when(late)
+    def _():
+        hailed(2)
+        planes_start()
+
     prepare(1)
     for k in range(n_chunks):
         receive(0, k, UP, DOWN)
         for f, h in cells:
             middle(k, f, h)
         send(1, k, Z)
-    hailed(2)
-    chips_start()
+
+    @pl.when(jnp.logical_not(late))
+    def _():
+        hailed(2)
+        planes_start()
 
     for k in range(n_chunks):
         receive(1, k, Z)
         conv(1, k)
-    scale = chips_end()
+    scale = planes_end()
     for k in range(n_chunks):
         receive(1, k, UP, DOWN)
         for f, h in cells:
@@ -357,14 +381,14 @@
                 for k in range(n_chunks):
                     copy(p, k, name).wait_send()
 
-    for q in range(3):
+    for q in range(2):
         for c in sum_copies(q):
             c.wait_send()
     for d in reach:
 
-        @pl.when(along(d)[1])
+        @pl.when(on_tm(d))
         def _():
-            chip_copy(d).wait_send()
+            plane_copy(d).wait_send()
 
     for k in range(n_chunks):
         store(k).wait()
@@ -374,24 +398,25 @@
     n_tm, n_rows = lax.axis_size("tm"), lax.axis_size("rows")
     frames, rows, chans, width = feats.shape
     nc = width // L
-    hbm = pl.BlockSpec(memory_space=pl.ANY)
-    vmem = pl.BlockSpec(memory_space=pltpu.VMEM)
-    smem = pl.BlockSpec(memory_space=pltpu.SMEM)
+    hbm = pl.BlockSpec(memory_space=pltpu.HBM)
     tall = 3 * chans
     return pl.pallas_call(
         functools.partial(kernel, n_tm, n_rows, 4, nc, chans),
         out_shape=jax.ShapeDtypeStruct(feats.shape, BF16),
-        in_specs=[hbm, vmem, hbm, vmem, vmem, hbm, hbm, smem],
-        out_specs=hbm,
+        in_specs=[hbm] * 8,
+        out_specs=pl.BlockSpec(memory_space=pl.ANY),
         scratch_shapes=[
             pltpu.VMEM(feats.shape, BF16),
+            pltpu.VMEM(gain.shape, F32),
+            pltpu.VMEM(out_gain.shape, F32),
+            pltpu.VMEM(rgb_weight.shape, F32),
+            pltpu.SMEM(frame_seg.shape, jnp.int32),
             pltpu.VMEM((frames, 3, rows, width), F32),
             pltpu.VMEM((frames, 3, rows, width), F32),
             pltpu.VMEM(conv_weight.shape, BF16),
-            pltpu.VMEM((2 * tall, 2 * tall), BF16),
-            pltpu.VMEM((2 * tall, tall), BF16),
-            pltpu.VMEM((2, 2, 2 * tall, 2 * tall), BF16),
-            pltpu.VMEM((2, 2, 2 * tall, tall), BF16),
+            pltpu.VMEM((2, 2 * tall, 2 * tall), BF16),
+            pltpu.VMEM((2, 2 * tall, tall), BF16),
+            pltpu.VMEM((nc, 3, rows, chans, 2 * L), BF16),
             pltpu.VMEM((5, chans, L), F32),
             pltpu.VMEM((nc, 4, 2, chans, L), BF16),
             pltpu.VMEM((nc, 4, 2, chans, L), BF16),
@@ -404,16 +429,16 @@
             pltpu.VMEM((2, nc, 2, 2, chans, L), BF16),
             pltpu.VMEM((2, nc, 2, 2, chans, L), BF16),
             pltpu.VMEM(feats.shape, BF16),
-            pltpu.VMEM((4, 4, 8, L), F32),
-            pltpu.VMEM((n_tm - 1, 8, L), F32),
-            pltpu.SemaphoreType.DMA((4,)),
+            pltpu.VMEM((3, 4, 8, L), F32),
+            pltpu.VMEM((2 * n_tm - 1, 8, L), F32),
+            pltpu.SemaphoreType.DMA((8,)),
             pltpu.SemaphoreType.DMA((nc,)),
             pltpu.SemaphoreType.DMA((2, nc, 3)),
             pltpu.SemaphoreType.DMA((2, nc, 3)),
-            pltpu.SemaphoreType.DMA((3, 3)),
-            pltpu.SemaphoreType.DMA((3, 3)),
-            pltpu.SemaphoreType.DMA((n_tm - 1,)),
-            pltpu.SemaphoreType.DMA((n_tm - 1,)),
+            pltpu.SemaphoreType.DMA((2, 3)),
+            pltpu.SemaphoreType.DMA((2, 3)),
+            pltpu.SemaphoreType.DMA((2 * n_tm - 1,)),
+            pltpu.SemaphoreType.DMA((2 * n_tm - 1,)),
             pltpu.SemaphoreType.REGULAR((3,)),
         ],
         compiler_params=pltpu.CompilerParams(

time: 36.7 us -> 34.1 us (0.929)
  the two profiles are of different devices: /device:TPU:1 before, /device:TPU:105 now
where the time goes in v3:
time: 34.1 us; the launch traced here: 34 us
  Pallas kernels  32.1 us (94%)
  local copies, waits for them, and re-layouts  1.85 us (5%)
    pallas_call x1, Pallas kernels, local(): pl.pallas_call(functools.partial(kernel, n_tm, n_rows, 4, nc, chans), out...  32.1 us
    unnamed x1, local copies, waits for them, and re-layouts  1.85 us

profile of v3, /device:TPU:105, one launch (start us, length us, event | category | flops | bytes accessed | tf_op | source)
XLA Modules:
  0.0 34.0 jit_solution(8445055907724729511)
XLA Ops:
  0.0 32.1 %shard_map.82 = bf16[2,2,96,640]{3,2,1,0:T(8,128)(2,1)} custom-call(bf16[2,2,96,640]{3,2,1,0:T(8,128)(2,1)} %feats_hbm.1, f32[96]{0:T(128)} %gain_hbm.1, bf16[96,2592]{1,0:T(8,128)(2,1)} %w_hbm.1, f32[96]{0:T(128)} %og_hbm.1, f32[3,96]{1,0:T(4,128)} %rgbw_hbm.1, f32[2,3,2,640]{3,2,1,0:T(2,128)} %bitcast.2, f32[2,3,2,640]{3,2,1,0:T(2,128)} %bitcast.3, s32[32]{0:T(128)} %seg_hbm.1), custom_call_target="tpu_custom_call" | custom-call | tf_op jit(solution)/shard_map/pallas_call | solution.py:403
  32.1 1.9 %copy.10 = bf16[2,2,96,640]{3,2,1,0:T(8,128)(2,1)} copy(bf16[2,2,96,640]{3,2,1,0:T(8,128)(2,1)} %shard_map.82) | data formatting | bytes 983040

commit v4 on v3

--- a/solution.py
+++ b/solution.py
@@ -339,17 +339,9 @@
         if k in (1, 3):
             hailed(k // 2)
             hail(k // 2 + 1)
-        if k == 2:
+        if k == 3:
             sum_end(0)
             sum_start(1)
-    sum_end(1)
-
-    late = t >= n_tm // 2
-
-    @pl.when(late)
-    def _():
-        hailed(2)
-        planes_start()
 
     prepare(1)
     for k in range(n_chunks):
@@ -358,10 +350,9 @@
             middle(k, f, h)
         send(1, k, Z)
 
-    @pl.when(jnp.logical_not(late))
-    def _():
-        hailed(2)
-        planes_start()
+    sum_end(1)
+    hailed(2)
+    planes_start()
 
     for k in range(n_chunks):
         receive(1, k, Z)
@@ -402,7 +393,7 @@
     tall = 3 * chans
     return pl.pallas_call(
         functools.partial(kernel, n_tm, n_rows, 4, nc, chans),
-        out_shape=jax.ShapeDtypeStruct(feats.shape, BF16),
+        out_shape=pltpu.VMEM(feats.shape, BF16),
         in_specs=[hbm] * 8,
         out_specs=pl.BlockSpec(memory_space=pl.ANY),
         scratch_shapes=[

time: 34.1 us -> 31.4 us (0.921)
  the two profiles are of different devices: /device:TPU:105 before, /device:TPU:57 now
where the time goes in v4:
time: 31.4 us; the launch traced here: 31.3 us
  Pallas kernels  30.5 us (97%)
  local copies, waits for them, and re-layouts  0.78 us (2%)
    pallas_call x1, Pallas kernels, local(): pl.pallas_call(functools.partial(kernel, n_tm, n_rows, 4, nc, chans), out...  30.5 us
    unnamed x1, local copies, waits for them, and re-layouts  0.78 us

profile of v4, /device:TPU:57, one launch (start us, length us, event | category | flops | bytes accessed | tf_op | source)
XLA Modules:
  0.0 31.3 jit_solution(6240362846815258827)
XLA Ops:
  0.0 30.5 %shard_map.82 = bf16[2,2,96,640]{3,2,1,0:T(8,128)(2,1)S(1)} custom-call(bf16[2,2,96,640]{3,2,1,0:T(8,128)(2,1)} %feats_hbm.1, f32[96]{0:T(128)} %gain_hbm.1, bf16[96,2592]{1,0:T(8,128)(2,1)} %w_hbm.1, f32[96]{0:T(128)} %og_hbm.1, f32[3,96]{1,0:T(4,128)} %rgbw_hbm.1, f32[2,3,2,640]{3,2,1,0:T(2,128)} %bitcast.2, f32[2,3,2,640]{3,2,1,0:T(2,128)} %bitcast.3, ...), custom_call_target="tpu_custom_call" | custom-call | tf_op jit(solution)/shard_map/pallas_call | solution.py:394
  30.5 0.8 %copy.10 = bf16[2,2,96,640]{3,2,1,0:T(8,128)(2,1)} copy(bf16[2,2,96,640]{3,2,1,0:T(8,128)(2,1)S(1)} %shard_map.82) | data formatting | bytes 983040

commit v5 on v4

--- a/solution.py
+++ b/solution.py
@@ -105,10 +105,10 @@
         if name == Z:
             buf = (act if p == 0 else grad).at[k]
             own, oth = (pl.ds(2, 2), pl.ds(0, 2)) if p == 0 else (pl.ds(0, 2), pl.ds(2, 2))
-            return remote(buf.at[own], buf.at[oth], s.at[Z], v.at[Z], (t + 1 - 2 * p, r))
+            return remote(buf.at[own], buf.at[oth], s.at[Z], v.at[Z], (lax.rem(t + n_tm + 1 - 2 * p, n_tm), r))
         if name == UP:
-            return remote(give.at[p, k, 0], take.at[p, k, 1], s.at[UP], v.at[UP], (t, r - 1))
-        return remote(give.at[p, k, 1], take.at[p, k, 0], s.at[DOWN], v.at[DOWN], (t, r + 1))
+            return remote(give.at[p, k, 0], take.at[p, k, 1], s.at[UP], v.at[UP], (t, lax.rem(r + n_rows - 1, n_rows)))
+        return remote(give.at[p, k, 1], take.at[p, k, 0], s.at[DOWN], v.at[DOWN], (t, lax.rem(r + 1, n_rows)))
 
     leaves = ({Z: not_last, UP: has_up, DOWN: has_down}, {Z: not_first, UP: has_up, DOWN: has_down})
     comes = ({Z: not_first, UP: has_down, DOWN: has_up}, {Z: not_last, UP: has_down, DOWN: has_up})
@@ -150,7 +150,7 @@
 
     def plane_copy(d):
         q = n_tm - 1 + d
-        return remote(zsum.at[n_tm - 1], zsum.at[q], zssem.at[q], zrsem.at[q], (t + d, r))
+        return remote(zsum.at[n_tm - 1], zsum.at[q], zssem.at[q], zrsem.at[q], (lax.rem(t + n_tm + d, n_tm), r))
 
     def planes_start():
         zsum[n_tm - 1] = wsum[2, 0]

time: 31.4 us -> 31.4 us (level)
  no operation moved by 1% of the time
where the time goes in v5:
time: 31.4 us; the launch traced here: 31.3 us
  Pallas kernels  30.5 us (97%)
  local copies, waits for them, and re-layouts  0.78 us (2%)
    pallas_call x1, Pallas kernels, local(): pl.pallas_call(functools.partial(kernel, n_tm, n_rows, 4, nc, chans), out...  30.5 us
    unnamed x1, local copies, waits for them, and re-layouts  0.78 us

profile of v5, /device:TPU:57, one launch (start us, length us, event | category | flops | bytes accessed | tf_op | source)
XLA Modules:
  0.0 31.3 jit_solution(10518418913360782339)
XLA Ops:
  0.0 30.5 %shard_map.82 = bf16[2,2,96,640]{3,2,1,0:T(8,128)(2,1)S(1)} custom-call(bf16[2,2,96,640]{3,2,1,0:T(8,128)(2,1)} %feats_hbm.1, f32[96]{0:T(128)} %gain_hbm.1, bf16[96,2592]{1,0:T(8,128)(2,1)} %w_hbm.1, f32[96]{0:T(128)} %og_hbm.1, f32[3,96]{1,0:T(4,128)} %rgbw_hbm.1, f32[2,3,2,640]{3,2,1,0:T(2,128)} %bitcast.2, f32[2,3,2,640]{3,2,1,0:T(2,128)} %bitcast.3, ...), custom_call_target="tpu_custom_call" | custom-call | tf_op jit(solution)/shard_map/pallas_call | solution.py:394
  30.5 0.8 %copy.10 = bf16[2,2,96,640]{3,2,1,0:T(8,128)(2,1)} copy(bf16[2,2,96,640]{3,2,1,0:T(8,128)(2,1)S(1)} %shard_map.82) | data formatting | bytes 983040

commit v6 on v5

--- a/solution.py
+++ b/solution.py
@@ -186,7 +186,7 @@
             for e in range(3):
                 for k in range(n_chunks):
                     weight = weight + jnp.sum(pix[f, e, :, k * L : (k + 1) * L], axis=0, keepdims=True)
-        wsum[0, 0] = jnp.broadcast_to(weight, (8, L))
+        wsum[0, 0] = weight
 
     loads["feats"].wait()
     for k in range(n_chunks):
@@ -420,8 +420,8 @@
             pltpu.VMEM((2, nc, 2, 2, chans, L), BF16),
             pltpu.VMEM((2, nc, 2, 2, chans, L), BF16),
             pltpu.VMEM(feats.shape, BF16),
-            pltpu.VMEM((3, 4, 8, L), F32),
-            pltpu.VMEM((2 * n_tm - 1, 8, L), F32),
+            pltpu.VMEM((3, 4, 1, L), F32),
+            pltpu.VMEM((2 * n_tm - 1, 1, L), F32),
             pltpu.SemaphoreType.DMA((8,)),
             pltpu.SemaphoreType.DMA((nc,)),
             pltpu.SemaphoreType.DMA((2, nc, 3)),

time: 31.4 us -> 30.8 us (0.981)
  Pallas kernels: 30.5 us -> 29.9 us
    pallas_call x1, Pallas kernels: 30.5 us -> 29.9 us  [local(): pl.pallas_call(functools.partial(kernel, n_tm, n_rows, 4, nc, chans), out...]
where the time goes in v6:
time: 30.8 us; the launch traced here: 30.7 us
  Pallas kernels  29.9 us (97%)
  local copies, waits for them, and re-layouts  0.78 us (3%)
    pallas_call x1, Pallas kernels, local(): pl.pallas_call(functools.partial(kernel, n_tm, n_rows, 4, nc, chans), out...  29.9 us
    unnamed x1, local copies, waits for them, and re-layouts  0.78 us

profile of v6, /device:TPU:57, one launch (start us, length us, event | category | flops | bytes accessed | tf_op | source)
XLA Modules:
  0.0 30.7 jit_solution(6875774392384466361)
XLA Ops:
  0.0 29.9 %shard_map.82 = bf16[2,2,96,640]{3,2,1,0:T(8,128)(2,1)S(1)} custom-call(bf16[2,2,96,640]{3,2,1,0:T(8,128)(2,1)} %feats_hbm.1, f32[96]{0:T(128)} %gain_hbm.1, bf16[96,2592]{1,0:T(8,128)(2,1)} %w_hbm.1, f32[96]{0:T(128)} %og_hbm.1, f32[3,96]{1,0:T(4,128)} %rgbw_hbm.1, f32[2,3,2,640]{3,2,1,0:T(2,128)} %bitcast.2, f32[2,3,2,640]{3,2,1,0:T(2,128)} %bitcast.3, ...), custom_call_target="tpu_custom_call" | custom-call | tf_op jit(solution)/shard_map/pallas_call | solution.py:394
  29.9 0.8 %copy.10 = bf16[2,2,96,640]{3,2,1,0:T(8,128)(2,1)} copy(bf16[2,2,96,640]{3,2,1,0:T(8,128)(2,1)S(1)} %shard_map.82) | data formatting | bytes 983040
